TPU v7x, 128 devices: a whole 4x4x4 slice. The times are simulated.
128 devices in a mesh: bins: 4 (over z), tiles: 32 (over y, x, core).
Axes of the slice: x: 4, y: 4, z: 4, core: 2. Of those that a mesh axis runs over, the one named last changes fastest.
Arguments:
- spectrum: float32 [1800, 256, 256], P('bins', 'tiles'), may hold values from 0.1 to 2
- speed: float32 [50], replicated, may hold values from 0.3 to 0.95
- quad_a: bfloat16 [1800, 1800], replicated, may hold values from -0.125 to 0.125
- quad_b: bfloat16 [1800, 1800], replicated, may hold values from -0.125 to 0.125
- growth: float32 [1800], replicated, may hold values from 0.05 to 0.5
- dissip: float32 [1800], replicated, may hold values from 0.05 to 0.5
- wind: float32 [128, 512], P(('bins', 'tiles')), may hold values from 0.3 to 3
- cell_slot: int32 [256, 256], P('tiles'), may hold values from -1 to 2047, as said below
Outputs:
- evolved: float32 [1800, 256, 256], P('bins', 'tiles')
Inputs may be any that keep to these rules, and one draw needn't show every extreme that they name: `cell_slot`: -1 on land; otherwise s * 16 + m, meaning that shard s holds this cell in slot m of the cell's tile; within one tile (rows t * 8 to t * 8 + 7) each value appears at most once, a shard's used slots of a tile are 0 up to some count, and some shard has all 16 slots used in every tile.
All inputs are finite; a program needn't handle non-finite values.
Results may differ from a plain program's by a relative error of at most 0.0011.
Values may be sent and summed in bfloat16 or wider, within the bound.
A program may use at most 128 MiB of HBM per device.

v0:
```python
import math

import jax
import jax.numpy as jnp
from jax import lax
from jax.sharding import PartitionSpec as P

time_step = 0.25


def extended(cells, sides, width):
    for axis, dim in sides:
        count = lax.axis_size(axis)
        ends = count - 1
        head = lax.slice_in_dim(cells, 0, width, axis=dim)
        tail = lax.slice_in_dim(cells, cells.shape[dim] - width, cells.shape[dim], axis=dim)
        cells = jnp.concatenate(
            [
                lax.ppermute(tail, axis, [(i, (i + 1) % count) for i in range(ends)]),
                cells,
                lax.ppermute(head, axis, [((i + 1) % count, i) for i in range(ends)]),
            ],
            axis=dim,
        )
    return cells


def courant(bins, speed, nfreq, ndir):
    direction = bins // nfreq
    freq = bins % nfreq
    theta = (direction.astype(jnp.float32) + 0.5) * (2.0 * math.pi / ndir)
    cosine = jnp.cos(theta)
    sine = jnp.sin(theta)
    total = jnp.abs(cosine) + jnp.abs(sine)
    rate = speed[freq]
    return (rate * cosine / total, rate * sine / total)


def advance(field, west, east, cour_x, cour_y, sea):
    cxb = cour_x[:, None, None]
    cyb = cour_y[:, None, None]
    ypad = jnp.pad(field, ((0, 0), (0, 0), (1, 1)))
    south = ypad[:, :, :-2]
    north = ypad[:, :, 2:]
    up_x = jnp.where(cxb > 0, west, east)
    up_y = jnp.where(cyb > 0, south, north)
    return (field - jnp.abs(cxb) * (field - up_x) - jnp.abs(cyb) * (field - up_y)) * sea


def on_device(spectrum, speed, quad_a, quad_b, growth, dissip, wind, cell_slot):
    groups = lax.axis_size("bins")
    tiles = lax.axis_size("tiles")
    group_bins = spectrum.shape[0]
    all_bins = group_bins * groups
    nfreq = speed.shape[0]
    ndir = all_bins // nfreq
    slot_count = wind.shape[1]
    most = slot_count // tiles
    first_bin = lax.axis_index("bins") * group_bins
    bins_here = first_bin + jnp.arange(group_bins, dtype=jnp.int32)
    cour_x, cour_y = courant(bins_here, speed, nfreq, ndir)
    sea = (cell_slot >= 0).astype(jnp.float32)[None]
    field = spectrum * sea
    padded = extended(field, (("tiles", 1),), 1)
    prop = advance(field, padded[:, :-2], padded[:, 2:], cour_x, cour_y, sea)
    sent_here = prop.astype(jnp.bfloat16)
    devices = groups * tiles
    flat = sent_here.reshape(group_bins, -1)
    flat_slot = cell_slot.reshape(-1)
    cell_count = flat_slot.shape[0]
    target = jnp.where(flat_slot >= 0, flat_slot, devices * most)
    listing = (
        jnp.full((devices * most,), -1, jnp.int32)
        .at[target]
        .set(jnp.arange(cell_count, dtype=jnp.int32), mode="drop")
    )
    picked = jnp.take(flat, jnp.maximum(listing, 0), axis=1)
    picked = jnp.where(listing[None, :] >= 0, picked, jnp.zeros_like(picked))
    received = lax.all_to_all(picked, ("bins", "tiles"), split_axis=1, concat_axis=1, tiled=True)
    received = received.reshape(group_bins, groups, slot_count)
    quad3_a = quad_a.reshape(groups, group_bins, all_bins)
    quad3_b = quad_b.reshape(groups, group_bins, all_bins)
    dims = (((0, 1), (1, 0)), ((), ()))
    pair_a = lax.dot_general(quad3_a, received, dims, preferred_element_type=jnp.float32).reshape(
        groups, group_bins, slot_count
    )
    pair_b = lax.dot_general(quad3_b, received, dims, preferred_element_type=jnp.float32).reshape(
        groups, group_bins, slot_count
    )
    mean_e = jnp.sum(received.astype(jnp.float32), axis=(0, 1)) / all_bins
    energy = jnp.transpose(received, (1, 0, 2)).astype(jnp.float32)
    grow = growth.reshape(groups, group_bins)[:, :, None]
    damp = dissip.reshape(groups, group_bins)[:, :, None]
    force = wind[0][None, None, :]
    total = pair_a * pair_b + grow * force * energy - damp * mean_e[None, None, :] * energy
    change = (time_step * total).astype(jnp.bfloat16)
    lookup = jnp.maximum(cell_slot, 0).reshape(-1)
    outgoing = jnp.transpose(change, (1, 0, 2)).reshape(group_bins, devices * most)
    returned = lax.all_to_all(outgoing, ("bins", "tiles"), split_axis=1, concat_axis=1, tiled=True)
    increment = jnp.take(returned, lookup, axis=1).reshape(prop.shape)
    return prop + increment.astype(jnp.float32) * sea


def solution(mesh):
    placed = (
        P("bins", "tiles", None),
        P(),
        P(),
        P(),
        P(),
        P(),
        P(("bins", "tiles"), None),
        P("tiles", None),
    )
    return jax.shard_map(
        on_device, mesh=mesh, in_specs=placed, out_specs=P("bins", "tiles", None), check_vma=False
    )
```

profile of v0, /device:TPU:0, one launch (start us, length us, event | category | flops | bytes accessed | tf_op | source)
XLA Modules:
  0.0 205.9 jit_solution(5639303228946875084)
XLA Ops:
  0.0 0.7 compare_convert_fusion
  0.7 0.0 copy-start.2
  0.7 0.0 copy-start.3
  0.7 3.2 %copy_multiply_fusion = f32[450,8,256]{2,0,1:T(8,128)S(1)} fusion(f32[450,8,256]{2,1,0:T(8,128)} %param.10, f32[8,256]{1,0:T(8,128)S(1)} %compare_convert_fusion), kind=kLoop, calls=%fused_computation.23 | loop fusion | flops 921600 | bytes 7380992 | tf_op jit(solution)/shard_map/mul | solution.py:63
  3.9 0.0 copy-start
  4.0 1.8 copy-done
  5.7 0.1 fusion.22
  5.8 1.3 collective-permute-start.1
  7.1 3.1 %collective-permute-start = (f32[450,1,256]{2,0,1:T(8,128)S(1)}, f32[450,1,256]{2,0,1:T(8,128)S(1)}, u32[]{:S(2)}, u32[]{:S(2)}) collective-permute-start(f32[450,1,256]{2,0,1:T(8,128)S(1)} %get-tuple-element.13), channel_id=1, source_target_pairs={{0,1},{1,2},{2,3},{3,4},{4,5},{5,6},{6,7},{7,8},{8,9},{9,10},{10,1... | collective-permute-start | bytes 1382408 | tf_op jit(solution)/shard_map/ppermute | solution.py:19
  11.1 0.0 copy-done.2
  11.1 0.7 fusion.25
  11.8 0.7 fusion.24
  12.6 0.7 fusion.23
  13.3 0.0 copy-done.3
  13.3 4.3 %compare_select_fusion.4 = f32[450,1]{0,1:T(1,128)S(1)} fusion(f32[]{:T(128)} %bitcast.43, f32[]{:T(128)} %bitcast.44, f32[]{:T(128)} %bitcast.45, f32[]{:T(128)} %bitcast.46, f32[]{:T(128)} %bitcast.47, f32[]{:T(128)} %bitcast.49, f32[]{:T(128)} %bitcast.48, s32[]{:T(128)S(6)} %mul.133), kind=kLoop, calls=%fused_computation.78 | loop fusion | flops 9900 | bytes 1832 | tf_op jit(solution)/shard_map/gather | solution.py:35
  17.6 26.8 %broadcast_compare_fusion.2 = (pred[450]{0:T(512)(128)(4,1)S(1)}, f32[450]{0:T(512)S(1)}, f32[450]{0:T(512)S(1)}) fusion(s32[]{:T(128)S(6)} %mul.133, pred[450]{0:T(512)(128)(4,1)S(1)} %get-tuple-element.67, pred[450]{0:T(512)(128)(4,1)S(1)} %get-tuple-element.68, pred[450]{0:T(512)(128)(4,1)S(1)} %get-tuple-element.69, ...), kind=kLoop, calls=%fused_computation.104 | loop fusion | flops 27450 | bytes 25376 | tf_op jit(solution)/shard_map/gt | solution.py:45
  44.5 0.1 broadcast_compare_fusion.1
  44.6 8.0 %scatter_custom_fusion = s32[2048]{0:T(1024)S(1)} fusion(s32[2048]{0:T(1024)S(1)} %bitcast.113, s32[2048]{0:T(1024)S(1)} %iota.19, s32[]{:T(128)} %constant.21.clone.1), kind=kCustom, calls=%fused_computation.90 | custom fusion | bytes 8196 | tf_op jit(solution)/shard_map/scatter | solution.py:75
  52.7 0.0 collective-permute-done.1
  52.7 0.0 collective-permute-done
  52.7 10.1 %fusion.20 = (bf16[450,8,256]{2,0,1:T(8,128)(2,1)}, f32[450,8,256]{2,0,1:T(8,128)}) fusion(f32[8,256]{1,0:T(8,128)S(1)} %compare_convert_fusion, f32[450,8,256]{2,0,1:T(8,128)} %copy-done, pred[450]{0:T(512)(128)(4,1)S(1)} %get-tuple-element.11, f32[450]{0:T(512)S(1)} %abs.51, f32[450,1,256]{2,0,1:T(8,128)S(1)} %collective-permute-done.1, ...), kind=kLoop, calls=%fused_computation.107 | loop fusion | flops 11059200 | bytes 10150292 | tf_op jit(solution)/shard_map/convert_element_type | solution.py:66
  62.8 2.8 %copy.17 = bf16[450,8,256]{0,2,1:T(8,128)(2,1)S(1)} copy(bf16[450,8,256]{2,0,1:T(8,128)(2,1)} %get-tuple-element.6) | data formatting | bytes 3686400 | tf_op jit(solution)/shard_map/convert_element_type | solution.py:66
  65.6 9.2 %gather_fusion = bf16[2048,450]{1,0:T(8,128)(2,1)} fusion(bf16[450,2048]{0,1:T(8,128)(2,1)S(1)} %bitcast.101, s32[2048]{0:T(1024)S(1)} %maximum_clamp_fusion), kind=kCustom, calls=%fused_computation.clone | custom fusion | bytes 3694592 | tf_op jit(solution)/shard_map/jit(_take)/gather | solution.py:77
  74.8 2.9 %bitcast_select_fusion = bf16[450,2048]{0,1:T(8,128)(2,1)} fusion(bf16[2048,450]{1,0:T(8,128)(2,1)} %gather_fusion, pred[2048]{0:T(1024)(128)(4,1)S(1)} %get-tuple-element.16, pred[2048]{0:T(1024)(128)(4,1)S(1)} %get-tuple-element.15), kind=kLoop, calls=%fused_computation.27 | loop fusion | flops 1843200 | bytes 3690496 | tf_op jit(solution)/shard_map/jit(_where)/select_n | solution.py:78
  77.7 13.8 %all-to-all-start = ((bf16[450,128,16]{0,2,1:T(8,128)(2,1)}), bf16[450,128,16]{0,2,1:T(8,128)(2,1)S(1)}, u32[]{:S(2)}, u32[]{:S(2)}) async-start(bf16[450,128,16]{0,2,1:T(8,128)(2,1)} %bitcast.105), calls=%async_computation | async-start | bytes 4194304 | tf_op jit(solution)/shard_map/all_to_all | solution.py:79
  91.5 7.9 %reshape.159 = bf16[4,450,1800]{2,1,0:T(8,128)(2,1)} reshape(bf16[1800,1800]{1,0:T(8,128)(2,1)} %param.12) | data formatting | bytes 12960000 | tf_op jit(solution)/shard_map/reshape | solution.py:81
  99.4 8.0 %reshape.160 = bf16[4,450,1800]{2,1,0:T(8,128)(2,1)} reshape(bf16[1800,1800]{1,0:T(8,128)(2,1)} %param.13) | data formatting | bytes 12960000 | tf_op jit(solution)/shard_map/reshape | solution.py:82
  107.4 0.0 copy-done.4
  107.4 0.1 mul.152
  107.5 0.0 copy-done.5
  107.5 0.1 mul.146
  107.6 14.1 %all-to-all-done = bf16[450,128,16]{0,2,1:T(8,128)(2,1)S(1)} async-done(((bf16[450,128,16]{0,2,1:T(8,128)(2,1)}), bf16[450,128,16]{0,2,1:T(8,128)(2,1)S(1)}, u32[]{:S(2)}, u32[]{:S(2)}) %all-to-all-start) | async-done | bytes 1843232 | tf_op jit(solution)/shard_map/all_to_all | solution.py:79
  121.7 7.3 %fusion.26 = f32[512,1800,1]{0,1,2:T(8,128)S(1)} fusion(bf16[450,4,512]{0,2,1:T(8,128)(2,1)S(1)} %bitcast.102, bf16[4,450,1800]{2,1,0:T(8,128)(2,1)} %reshape.159), kind=kOutput, calls=%fused_computation.112 | convolution fusion | flops 3317760000 | bytes 12009600 | tf_op jit(solution)/shard_map/dot_general | solution.py:84
  129.1 0.0 copy-done.1
  129.1 6.4 %fusion.13 = f32[1800,512]{1,0:T(8,128)} fusion(f32[512,1800,1]{0,1,2:T(8,128)S(1)} %fusion.26, bf16[450,4,512]{0,2,1:T(8,128)(2,1)S(1)} %bitcast.103, bf16[4,450,1800]{2,1,0:T(8,128)(2,1)S(1)} %copy-done.1), kind=kOutput, calls=%fused_computation.26 | convolution fusion | flops 3318681600 | bytes 15696000 | tf_op jit(solution)/shard_map/dot_general | solution.py:87
  135.5 4.3 %mul.145 = f32[4,450,512]{2,1,0:T(8,128)} reshape(f32[1800,512]{1,0:T(8,128)} %fusion.13) | data formatting | bytes 7372800 | tf_op jit(solution)/shard_map/mul | solution.py:95
  139.8 5.1 %copy.20 = f32[4,450,512]{1,2,0:T(8,128)} copy(f32[4,450,512]{2,1,0:T(8,128)} %mul.145) | data formatting | bytes 7372800 | tf_op jit(solution)/shard_map/mul | solution.py:95
  145.0 0.4 convert_reduce_fusion
  145.3 0.1 reduce_sum.14
  145.5 0.0 copy-done.6
  145.5 5.0 %fusion.3 = bf16[4,450,512]{1,2,0:T(8,128)(2,1)} fusion(f32[4,450,512]{1,2,0:T(8,128)} %copy.20, f32[512]{0:T(512)S(1)} %broadcast_multiply_fusion, f32[4,450]{1,0:T(4,128)S(1)} %mul.152, f32[512]{0:T(512)S(1)} %bitcast.114, f32[4,450]{1,0:T(4,128)S(1)} %mul.146, bf16[450,4,512]{0,2,1:T(8,128)(2,1)S(1)} %bitcast.104), kind=kLoop, calls=%fused_computation.10 | loop fusion | flops 8294400 | bytes 7391296 | tf_op jit(solution)/shard_map/convert_element_type | solution.py:96
  150.4 4.7 %all-to-all-start.1 = ((bf16[450,128,16]{0,2,1:T(8,128)(2,1)}), bf16[450,128,16]{0,2,1:T(8,128)(2,1)S(1)}, u32[]{:S(2)}, u32[]{:S(2)}) async-start(bf16[450,128,16]{0,2,1:T(8,128)(2,1)} %bitcast.106), calls=%async_computation.1 | async-start | bytes 4194304 | tf_op jit(solution)/shard_map/all_to_all | solution.py:99
  155.1 30.3 %all-to-all-done.1 = bf16[450,128,16]{0,2,1:T(8,128)(2,1)S(1)} async-done(((bf16[450,128,16]{0,2,1:T(8,128)(2,1)}), bf16[450,128,16]{0,2,1:T(8,128)(2,1)S(1)}, u32[]{:S(2)}, u32[]{:S(2)}) %all-to-all-start.1) | async-done | bytes 1843232 | tf_op jit(solution)/shard_map/all_to_all | solution.py:99
  185.5 9.2 %gather_fusion.1 = bf16[2048,450]{1,0:T(8,128)(2,1)} fusion(bf16[450,2048]{0,1:T(8,128)(2,1)S(1)} %bitcast.100, s32[2048]{0:T(1024)S(1)} %fusion.14), kind=kCustom, calls=%fused_computation.1.clone | custom fusion | bytes 3694592 | tf_op jit(solution)/shard_map/jit(_take)/gather | solution.py:100
  194.7 1.8 broadcast_select_fusion
  196.4 2.7 %copy.21 = f32[450,8,256]{2,0,1:T(8,128)} copy(bf16[450,8,256]{0,2,1:T(8,128)(2,1)S(1)} %bitcast.107) | data formatting | bytes 5529600 | tf_op jit(solution)/shard_map/convert_element_type | solution.py:101
  199.2 3.7 %multiply_add_fusion = f32[450,8,256]{2,0,1:T(8,128)S(1)} fusion(f32[450,8,256]{2,0,1:T(8,128)} %get-tuple-element.7, f32[450,8,256]{2,0,1:T(8,128)} %copy.21, f32[8,256]{1,0:T(8,128)S(1)} %compare_convert_fusion), kind=kLoop, calls=%fused_computation.24 | loop fusion | flops 1843200 | bytes 11067392 | tf_op jit(solution)/shard_map/add | solution.py:101
  202.9 3.0 %copy.22 = f32[450,8,256]{2,1,0:T(8,128)} copy(f32[450,8,256]{2,0,1:T(8,128)S(1)} %multiply_add_fusion) | data formatting | bytes 7372800 | tf_op jit(solution)/shard_map/add | solution.py:101
  (39 shorter events, 1.0 us)
Async XLA Ops:
  0.7 10.4 %copy-start.2 = (f32[50]{0:T(128)S(1)}, f32[50]{0:T(128)}, u32[]{:S(2)}) copy-start(f32[50]{0:T(128)} %param.11) | copy-start | bytes 604
  0.7 12.6 %copy-start.3 = (s32[8,256]{1,0:T(8,128)S(1)}, s32[8,256]{1,0:T(8,128)}, u32[]{:S(2)}) copy-start(s32[8,256]{1,0:T(8,128)} %param.17) | copy-start | bytes 24580
  3.9 1.8 copy-start
  5.8 46.8 %collective-permute-start.1 = (f32[450,1,256]{2,0,1:T(8,128)S(1)}, f32[450,1,256]{2,0,1:T(8,128)S(1)}, u32[]{:S(2)}, u32[]{:S(2)}) collective-permute-start(f32[450,1,256]{2,0,1:T(8,128)S(1)} %get-tuple-element.14), channel_id=1, source_target_pairs={{1,0},{2,1},{3,2},{4,3},{5,4},{6,5},{7,6},{8,7},{9,8},{10,9},{11,1... | collective-permute-start | bytes 1382408 | tf_op jit(solution)/shard_map/ppermute | solution.py:21
  7.1 45.6 %collective-permute-start = (f32[450,1,256]{2,0,1:T(8,128)S(1)}, f32[450,1,256]{2,0,1:T(8,128)S(1)}, u32[]{:S(2)}, u32[]{:S(2)}) collective-permute-start(f32[450,1,256]{2,0,1:T(8,128)S(1)} %get-tuple-element.13), channel_id=1, source_target_pairs={{0,1},{1,2},{2,3},{3,4},{4,5},{5,6},{6,7},{7,8},{8,9},{9,10},{10,1... | collective-permute-start | bytes 1382408 | tf_op jit(solution)/shard_map/ppermute | solution.py:19
  77.7 44.0 %all-to-all-start = ((bf16[450,128,16]{0,2,1:T(8,128)(2,1)}), bf16[450,128,16]{0,2,1:T(8,128)(2,1)S(1)}, u32[]{:S(2)}, u32[]{:S(2)}) async-start(bf16[450,128,16]{0,2,1:T(8,128)(2,1)} %bitcast.105), calls=%async_computation | async-start | bytes 4194304 | tf_op jit(solution)/shard_map/all_to_all | solution.py:79
  99.4 8.0 %copy-start.4 = (f32[1800]{0:T(1024)S(1)}, f32[1800]{0:T(1024)}, u32[]{:S(2)}) copy-start(f32[1800]{0:T(1024)} %param.15) | copy-start | bytes 21604
  99.4 8.1 %copy-start.5 = (f32[1800]{0:T(1024)S(1)}, f32[1800]{0:T(1024)}, u32[]{:S(2)}) copy-start(f32[1800]{0:T(1024)} %param.14) | copy-start | bytes 21604
  121.7 7.4 %copy-start.1 = (bf16[4,450,1800]{2,1,0:T(8,128)(2,1)S(1)}, bf16[4,450,1800]{2,1,0:T(8,128)(2,1)}, u32[]{:S(2)}) copy-start(bf16[4,450,1800]{2,1,0:T(8,128)(2,1)} %reshape.160) | copy-start | bytes 19440004
  139.8 5.6 %copy-start.6 = (f32[1,512]{1,0:T(1,128)S(1)}, f32[1,512]{1,0:T(1,128)}, u32[]{:S(2)}) copy-start(f32[1,512]{1,0:T(1,128)} %param.16) | copy-start | bytes 6148
  150.4 35.0 %all-to-all-start.1 = ((bf16[450,128,16]{0,2,1:T(8,128)(2,1)}), bf16[450,128,16]{0,2,1:T(8,128)(2,1)S(1)}, u32[]{:S(2)}, u32[]{:S(2)}) async-start(bf16[450,128,16]{0,2,1:T(8,128)(2,1)} %bitcast.106), calls=%async_computation.1 | async-start | bytes 4194304 | tf_op jit(solution)/shard_map/all_to_all | solution.py:99
where the time goes:
time: 207 us; the launch traced here: 206 us
  local copies, waits for them, and re-layouts  64.6 us (31%)
  other arithmetic  59.9 us (29%)
  waiting for transfers between devices  44.5 us (21%)
  starting transfers between devices  22.8 us (11%)
  matrix products  13.8 us (7%)
    all_to_all x1, waiting for transfers between devices, on_device(): lax.all_to_all(outgoing, ('bins', 'tiles'), split_axis=1, concat_axis=1,...  30.3 us
    gt x1, other arithmetic, advance(): up_x = jnp.where(cxb > 0, west, east)  26.8 us
    all_to_all x1, waiting for transfers between devices, on_device(): lax.all_to_all(picked, ('bins', 'tiles'), split_axis=1, concat_axis=1, ti...  14.1 us
    all_to_all x1, starting transfers between devices, on_device(): lax.all_to_all(picked, ('bins', 'tiles'), split_axis=1, concat_axis=1, ti...  13.8 us
    convert_element_type x1, other arithmetic, on_device(): sent_here = prop.astype(jnp.bfloat16)  10.1 us
    mul x2, local copies, waits for them, and re-layouts, on_device(): pair_a * pair_b + grow * force * energy  9.44 us
    gather x1, local copies, waits for them, and re-layouts, on_device(): picked = jnp.take(flat, jnp.maximum(listing, 0), axis=1)  9.21 us
    gather x1, local copies, waits for them, and re-layouts, on_device(): increment = jnp.take(returned, lookup, axis=1).reshape(prop.shape)  9.2 us
  transfers between devices with their start and end apart: 4, of which 2 were waited for; matrix products, arithmetic and copies ran while one was open for 28% of the time, Pallas kernels for 0%

commit v1 on v0

v1 whole, which is shorter than its diff:
```python
import functools
import math

import jax
import jax.numpy as jnp
import numpy as np
from jax import lax
from jax.experimental import pallas as pl
from jax.experimental.pallas import tpu as pltpu
from jax.sharding import PartitionSpec as P

MESH = pl.DeviceIdType.MESH
F32 = jnp.float32
BF16 = jnp.bfloat16

GROUPS = 4
TILES = 32
OWN = 450
STEP = 448
WIN = 464
BINS = 1800
ROWS = 8
COLS = 256
CELLS = 2 * COLS
MOST = 16
SUB = 16
NT = (((1,), (1,)), ((), ()))


def kernel(
    cap,
    parts,
    spec,
    quad_a,
    quad_b,
    coef,
    wind,
    slot,
    out,
    most,
    field,
    qa,
    qb,
    sea,
    place,
    onehot,
    halo_out,
    halo_in,
    prop,
    sent,
    ahead,
    held,
    heldt,
    pairs,
    pairst,
    back,
    got,
    inc,
    wp,
    wy,
    wx,
    wc,
    wz,
    table,
    load_sem,
    halo_sem,
    fwd_send,
    fwd_recv,
    ret_send,
    ret_recv,
    wind_send,
    wind_recv,
):
    z = lax.axis_index("bins")
    t = lax.axis_index("tiles")
    ty = t // 8
    tx = (t // 2) % 4
    tc = t % 2
    west = 1 - ((z + 1) // 2) % 2
    turn = 2 * west - 1
    count = WIN // SUB

    for h in range(2):
        field[h, 0:8] = jnp.zeros((8, ROWS, 128), F32)
        field[h, STEP:WIN] = jnp.zeros((WIN - STEP, ROWS, 128), F32)
    load_x = [
        pltpu.make_async_copy(
            spec.at[:, :, pl.ds(128 * h, 128)], field.at[h, pl.ds(2 * z, OWN)], load_sem.at[h]
        )
        for h in range(2)
    ]
    for load in load_x:
        load.start()
    load_a = pltpu.make_async_copy(quad_a, qa, load_sem.at[2])
    load_b = pltpu.make_async_copy(quad_b, qb, load_sem.at[3])
    load_a.start()
    load_b.start()

    barrier = pltpu.get_barrier_semaphore()
    peers = [(lax.rem(z + i, 4), t) for i in (1, 2, 3)]
    peers += [(z, lax.rem(t + 1, TILES)), (z, lax.rem(t + TILES - 1, TILES))]
    ypeers = [lax.rem(ty + i, 4) for i in (1, 2, 3)]
    xpeers = [lax.rem(tx + i, 4) for i in (1, 2, 3)]
    peers += [(z, p * 8 + lax.rem(t, 8)) for p in ypeers]
    peers += [(z, ty * 8 + p * 2 + tc) for p in xpeers]
    for peer in peers:
        pl.semaphore_signal(barrier, inc=1, device_id=peer, device_id_type=MESH)

    wet = (slot[...] >= 0).astype(F32)
    sea[...] = wet
    left = lax.broadcasted_iota(jnp.int32, (COLS, COLS), 0)
    right = lax.broadcasted_iota(jnp.int32, (COLS, COLS), 1)
    upto = (left <= right).astype(F32).astype(BF16)
    running = jnp.dot(wet.astype(BF16), upto, preferred_element_type=F32)
    total = jnp.sum(wet, axis=1, keepdims=True)
    before = pltpu.roll(jnp.broadcast_to(total, (ROWS, COLS)), 1, 0)
    odd = lax.broadcasted_iota(jnp.int32, (ROWS, COLS), 0) % 2 == 1
    running = running + jnp.where(odd, before, 0.0)
    place[...] = jnp.where(wet > 0, running - 1.0, -1.0)
    fullest = jnp.max(running)

    held[:, WIN:512, :] = jnp.zeros((GROUPS, 512 - WIN, cap), BF16)
    pairs[:, 1792:1920] = jnp.zeros((pairs.shape[0], 128), BF16)

    flat = field.reshape(2 * WIN * ROWS, 128)

    def strip(i, r):
        base = i * (SUB * ROWS) + r
        return [pl.ds(h * (WIN * ROWS) + base, SUB, stride=ROWS) for h in range(2)]

    def take(i, r):
        return jnp.concatenate([flat[at, :] for at in strip(i, r)], axis=1)

    def put(i, r, value):
        for h, at in enumerate(strip(i, r)):
            flat[at, :] = value[:, 128 * h : 128 * h + 128]

    for load in load_x:
        load.wait()
    edge = 7 * west
    edge_sea = sea[pl.ds(edge, 1), :]

    def halo_step(i, carry):
        v = take(i, edge)
        halo_out[pl.ds(pl.multiple_of(i * SUB, SUB), SUB), :] = v * edge_sea
        return carry

    lax.fori_loop(0, count, halo_step, 0)
    pl.semaphore_wait(barrier, len(peers))
    halo = pltpu.make_async_remote_copy(
        src_ref=halo_out,
        dst_ref=halo_in,
        send_sem=halo_sem.at[0],
        recv_sem=halo_sem.at[1],
        device_id=(z, lax.rem(t + turn + TILES, TILES)),
        device_id_type=MESH,
    )
    halo.start()
    outer = (1 - west) * (TILES - 1)
    halo_there = (t != outer).astype(F32)

    lane = lax.broadcasted_iota(jnp.int32, (SUB, COLS), 1)
    south = z < 2
    shift = jnp.where(south, 1, COLS - 1)
    wall = lane == jnp.where(south, 0, COLS - 1)
    from_west = west == 1

    def propagate(g, edged):
        r0 = 2 * g
        ru = jnp.clip(r0 + 2 - 3 * west, 0, ROWS - 1)
        sea0 = sea[pl.ds(r0, 1), :]
        sea1 = sea[pl.ds(r0 + 1, 1), :]
        seau = sea[pl.ds(ru, 1), :]
        at_edge = g == (1 - west) * (GROUPS - 1)

        def step(i, carry):
            here = pl.ds(pl.multiple_of(i * SUB, SUB), SUB)
            f0 = take(i, r0) * sea0
            f1 = take(i, r0 + 1) * sea1
            fu = take(i, ru) * seau
            if edged:
                fu = jnp.where(at_edge, halo_in[here, :] * halo_there, fu)
            consts = coef[pl.ds(pl.multiple_of(z * STEP + i * SUB, SUB), SUB), :]
            cx = consts[:, 0:1]
            cy = consts[:, 1:2]
            up0 = jnp.where(from_west, fu, f1)
            up1 = jnp.where(from_west, f0, fu)
            y0 = jnp.where(wall, 0.0, pltpu.roll(f0, shift, 1))
            y1 = jnp.where(wall, 0.0, pltpu.roll(f1, shift, 1))
            p0 = (f0 - cx * (f0 - up0) - cy * (f0 - y0)) * sea0
            p1 = (f1 - cx * (f1 - up1) - cy * (f1 - y1)) * sea1
            prop[g, here, 0:COLS] = p0
            prop[g, here, COLS:CELLS] = p1
            sent[here, 0:COLS] = p0.astype(BF16)
            sent[here, COLS:CELLS] = p1.astype(BF16)
            return carry

        lax.fori_loop(0, count, step, 0)
        rank = lax.broadcasted_iota(jnp.int32, (cap, COLS), 0).astype(F32)
        onehot[g, :, 0:COLS] = jnp.where(rank == place[pl.ds(r0, 1), :], 1.0, 0.0).astype(BF16)
        onehot[g, :, COLS:CELLS] = jnp.where(rank == place[pl.ds(r0 + 1, 1), :], 1.0, 0.0).astype(BF16)
        return lax.dot_general(sent[...], onehot[g], NT, preferred_element_type=F32).astype(BF16)

    late = z // 3
    order = [
        1 + lax.rem(z, 2),
        2 * (1 - (z + 2) // 3) + late,
        3 * (1 - late),
        z,
    ]

    starts = [sum(parts[:i]) for i in range(len(parts))]

    def forward(i, c):
        return pltpu.make_async_remote_copy(
            src_ref=ahead.at[i, :, pl.ds(starts[c], parts[c])],
            dst_ref=held.at[z, pl.ds(0, WIN), pl.ds(starts[c], parts[c])],
            send_sem=fwd_send.at[c, i],
            recv_sem=fwd_recv.at[c, z],
            device_id=(order[i], t),
            device_id_type=MESH,
        )

    for i in range(3):
        if i == 2:
            halo.wait()
        ahead[i] = propagate(order[i], i == 2)
        forward(i, 0).start()
    for c in range(1, len(parts)):
        for i in range(3):
            forward(i, c).start()
    held[z, 0:WIN, :] = propagate(z, True)

    mark = lax.broadcasted_iota(jnp.int32, (1, 128), 1)
    for p in range(TILES):
        row = wind[:, 128 * (p // 8) : 128 * (p // 8) + 128]
        if p % 8:
            row = pltpu.roll(row, 128 - MOST * (p % 8), 1)
        wp[p // 8, (p // 2) % 4, p % 2] = jnp.where(mark == MOST, fullest, row)
    wy[ty] = wp[ty]

    def wind_copy(k, src, dst, there):
        return pltpu.make_async_remote_copy(
            src_ref=src,
            dst_ref=dst,
            send_sem=wind_send.at[k],
            recv_sem=wind_recv.at[k],
            device_id=there,
            device_id_type=MESH,
        )

    def wind_y():
        return [
            wind_copy(i, wp.at[p], wy.at[ty], (z, p * 8 + lax.rem(t, 8))) for i, p in enumerate(ypeers)
        ]

    def wind_x():
        return [
            wind_copy(3 + i, wy.at[:, p], wx.at[tx], (z, ty * 8 + p * 2 + tc)) for i, p in enumerate(xpeers)
        ]

    def wind_c():
        return [wind_copy(6, wx.at[:, :, 1 - tc], wc.at[tc], (z, t + 1 - 2 * tc))]

    def wind_z():
        return [
            wind_copy(7 + i, wc, wz.at[z], (lax.rem(z + 1 + i, 4), t)) for i in range(3)
        ]

    def wind_next(stage):
        if stage == 0:
            for copy in wind_y():
                copy.start()
        if stage == 1:
            for copy in wind_y():
                copy.wait()
            wx[tx] = wy[:, tx]
            for copy in wind_x():
                copy.start()
        if stage == 2:
            for copy in wind_x():
                copy.wait()
            wc[tc] = wx[:, :, tc]
            for copy in wind_c():
                copy.start()
        if stage == 3:
            for copy in wind_c():
                copy.wait()
            wz[z] = wc[...]
            for copy in wind_z():
                copy.start()
        if stage == 4:
            for copy in wind_z():
                copy.wait()
            for i in range(128):
                table[i : i + 1, :] = wz[i // 32, (i // 16) % 2, (i // 4) % 4, i % 4]

    wind_next(0)

    load_a.wait()
    load_b.wait()

    def returning(i, c):
        h = lax.rem(z + i + 1, 4)
        return pltpu.make_async_remote_copy(
            src_ref=back.at[h, :, pl.ds(starts[c], parts[c])],
            dst_ref=got.at[z, :, pl.ds(starts[c], parts[c])],
            send_sem=ret_send.at[c, i],
            recv_sem=ret_recv.at[c, z],
            device_id=(h, t),
            device_id_type=MESH,
        )

    def landing(c, i):
        g = lax.rem(z + i + 1, 4)
        return pltpu.make_async_remote_copy(
            src_ref=ahead.at[i, :, pl.ds(starts[c], parts[c])],
            dst_ref=held.at[g, pl.ds(0, WIN), pl.ds(starts[c], parts[c])],
            send_sem=fwd_send.at[c, i],
            recv_sem=fwd_recv.at[c, g],
            device_id=(g, t),
            device_id_type=MESH,
        )

    def homing(c, i):
        g = lax.rem(z + i + 1, 4)
        return pltpu.make_async_remote_copy(
            src_ref=back.at[g, :, pl.ds(starts[c], parts[c])],
            dst_ref=got.at[g, :, pl.ds(starts[c], parts[c])],
            send_sem=ret_send.at[c, i],
            recv_sem=ret_recv.at[c, g],
            device_id=(g, t),
            device_id_type=MESH,
        )

    for c, n in enumerate(parts):
        at = pl.ds(starts[c], n)
        for i in range(3):
            landing(c, i).wait_recv()
        wind_next(1 + c)
        ones = jnp.ones((SUB, 512), BF16)
        mean = jnp.zeros((SUB, n), F32)
        for s in range(GROUPS):
            block = held[s, :, starts[c] : starts[c] + n]
            mean = mean + jnp.dot(ones, block, preferred_element_type=F32)
            heldt[0:n, 512 * s : 512 * s + 512] = block.T
        mean = mean / BINS
        for k0 in range(0, BINS, 512):
            k1 = min(k0 + 512, BINS)
            sums = []
            for q in (qa, qb):
                acc = None
                for s in range(GROUPS):
                    deep = min(WIN, BINS - STEP * s)
                    term = jnp.dot(
                        heldt[0:n, 512 * s : 512 * s + deep],
                        q[STEP * s : STEP * s + deep, k0:k1],
                        preferred_element_type=F32,
                    )
                    acc = term if acc is None else acc + term
                sums.append(acc)
            pairs[0:n, k0:k1] = (0.25 * (sums[0] * sums[1])).astype(BF16)
        for j in range(15):
            pairst[128 * j : 128 * j + 128, 0:n] = pairs[0:n, 128 * j : 128 * j + 128].T
        row = lax.broadcasted_iota(jnp.int32, (SUB, n), 0)
        high = mean.astype(BF16).astype(F32)
        mid = (mean - high).astype(BF16).astype(F32)
        low = mean - high - mid
        for h in range(GROUPS):
            back[h, 0:STEP, at] = pairst[STEP * h : STEP * h + STEP, 0:n]
            tail = pairst[STEP * h + STEP : STEP * h + WIN, 0:n].astype(F32)
            tail = jnp.where(row == 8, high, tail)
            tail = jnp.where(row == 9, mid, tail)
            tail = jnp.where(row == 10, low, tail)
            back[h, STEP:WIN, at] = tail.astype(BF16)
        for i in range(3):
            returning(i, c).start()

    for stage in range(1 + len(parts), 5):
        wind_next(stage)
    most[...] = jnp.broadcast_to(jnp.max(table[:, MOST : MOST + 1]), (8, 128))

    wide = table[...]
    w_high = wide.astype(BF16)
    w_mid = (wide - w_high.astype(F32)).astype(BF16)
    w_low = (wide - w_high.astype(F32) - w_mid.astype(F32)).astype(BF16)
    eye = (
        lax.broadcasted_iota(jnp.int32, (MOST, 128), 0) == lax.broadcasted_iota(jnp.int32, (MOST, 128), 1)
    ).astype(F32).astype(BF16)
    tables = [
        lax.dot_general(eye, w, NT, preferred_element_type=F32).astype(BF16) for w in (w_high, w_mid, w_low)
    ]

    def wind_row(r):
        cells = slot[pl.ds(r, 1), :]
        shard = cells // MOST
        line = (shard // 32) * 32 + (shard % 2) * 16 + ((shard // 2) % 4) * 4 + (shard // 8) % 4
        pick = lax.broadcasted_iota(jnp.int32, (128, COLS), 0) == line
        pick = jnp.where(pick, 1.0, 0.0).astype(BF16)
        found = sum(jnp.dot(w, pick, preferred_element_type=F32) for w in tables)
        here = lax.broadcasted_iota(jnp.int32, (MOST, COLS), 0) == cells % MOST
        return jnp.sum(jnp.where(here, found, 0.0), axis=0, keepdims=True)

    def finish(g, source):
        r0 = 2 * g
        inc[...] = jnp.dot(source[g], onehot[g], preferred_element_type=F32)
        means = jnp.sum(inc[STEP + 8 : STEP + 11, :], axis=0, keepdims=True)
        m0 = means[:, 0:COLS]
        m1 = means[:, COLS:CELLS]
        w0 = wind_row(r0)
        w1 = wind_row(r0 + 1)

        def step(i, carry):
            here = pl.ds(pl.multiple_of(i * SUB, SUB), SUB)
            consts = coef[pl.ds(pl.multiple_of(z * STEP + i * SUB, SUB), SUB), :]
            grow = consts[:, 2:3]
            damp = consts[:, 3:4]
            p0 = prop[g, here, 0:COLS]
            p1 = prop[g, here, COLS:CELLS]
            s0 = p0.astype(BF16).astype(F32)
            s1 = p1.astype(BF16).astype(F32)
            e0 = p0 + inc[here, 0:COLS] + (grow * w0 - damp * m0) * s0
            e1 = p1 + inc[here, COLS:CELLS] + (grow * w1 - damp * m1) * s1
            put(i, r0, e0)
            put(i, r0 + 1, e1)
            return carry

        lax.fori_loop(0, count, step, 0)

    finish(z, back)
    for i in range(3):
        for c in range(len(parts)):
            homing(c, i).wait_recv()
        finish(lax.rem(z + i + 1, 4), got)
    stores = [
        pltpu.make_async_copy(
            field.at[h, pl.ds(2 * z, OWN)], out.at[:, :, pl.ds(128 * h, 128)], load_sem.at[h]
        )
        for h in range(2)
    ]
    for store in stores:
        store.start()
    for i in range(3):
        for c in range(len(parts)):
            forward(i, c).wait_send()
            returning(i, c).wait_send()
    for store in stores:
        store.wait()


def coupled(cap, parts, cid, spectrum, quad_a, quad_b, coef, wind, slot):
    vmem = pl.BlockSpec(memory_space=pltpu.VMEM)
    hbm = pl.BlockSpec(memory_space=pl.ANY)
    n = len(parts)
    wide = max(parts)
    dma = pltpu.SemaphoreType.DMA
    return pl.pallas_call(
        functools.partial(kernel, cap, parts),
        out_shape=[
            jax.ShapeDtypeStruct(spectrum.shape, F32),
            jax.ShapeDtypeStruct((8, 128), F32),
        ],
        in_specs=[hbm, hbm, hbm, vmem, vmem, vmem],
        out_specs=[hbm, vmem],
        scratch_shapes=[
            pltpu.VMEM((2, WIN, ROWS, 128), F32),
            pltpu.VMEM((BINS, BINS), BF16),
            pltpu.VMEM((BINS, BINS), BF16),
            pltpu.VMEM((ROWS, COLS), F32),
            pltpu.VMEM((ROWS, COLS), F32),
            pltpu.VMEM((GROUPS, cap, CELLS), BF16),
            pltpu.VMEM((WIN, COLS), F32),
            pltpu.VMEM((WIN, COLS), F32),
            pltpu.VMEM((GROUPS, WIN, CELLS), F32),
            pltpu.VMEM((WIN, CELLS), BF16),
            pltpu.VMEM((3, WIN, cap), BF16),
            pltpu.VMEM((GROUPS, 512, cap), BF16),
            pltpu.VMEM((wide, GROUPS * 512), BF16),
            pltpu.VMEM((wide, 1920), BF16),
            pltpu.VMEM((1920, wide), BF16),
            pltpu.VMEM((GROUPS, WIN, cap), BF16),
            pltpu.VMEM((GROUPS, WIN, cap), BF16),
            pltpu.VMEM((WIN, CELLS), F32),
            pltpu.VMEM((4, 4, 2, 1, 128), F32),
            pltpu.VMEM((4, 4, 2, 1, 128), F32),
            pltpu.VMEM((4, 4, 2, 1, 128), F32),
            pltpu.VMEM((2, 4, 4, 1, 128), F32),
            pltpu.VMEM((4, 2, 4, 4, 1, 128), F32),
            pltpu.VMEM((128, 128), F32),
            dma((4,)),
            dma((2,)),
            dma((n, 3)),
            dma((n, 4)),
            dma((n, 3)),
            dma((n, 4)),
            dma((10,)),
            dma((10,)),
        ],
        compiler_params=pltpu.CompilerParams(
            collective_id=cid, has_side_effects=True, vmem_limit_bytes=56 << 20
        ),
        name="coupled%d" % cap,
    )(spectrum, quad_a, quad_b, coef, wind, slot)


def directions():
    theta = (np.arange(36) + 0.5) * (2.0 * math.pi / 36)
    cosine = np.abs(np.cos(theta))
    sine = np.abs(np.sin(theta))
    return cosine / (cosine + sine), sine / (cosine + sine)


def on_device(spectrum, speed, quad_a, quad_b, growth, dissip, wind, cell_slot):
    along, across = directions()
    cx = (jnp.asarray(along, F32)[:, None] * speed[None, :]).reshape(BINS)
    cy = (jnp.asarray(across, F32)[:, None] * speed[None, :]).reshape(BINS)
    coef = jnp.stack([cx, cy, 0.25 * growth, 0.25 * dissip], axis=1)
    coef = jnp.pad(coef, ((0, 8), (0, 0)))
    out, most = coupled(512, (256, 256), 0, spectrum, quad_a, quad_b, coef, wind, cell_slot)
    return out


def solution(mesh):
    placed = (
        P("bins", "tiles", None),
        P(),
        P(),
        P(),
        P(),
        P(),
        P(("bins", "tiles"), None),
        P("tiles", None),
    )
    return jax.shard_map(
        on_device, mesh=mesh, in_specs=placed, out_specs=P("bins", "tiles", None), check_vma=False
    )
```

time: 207 us -> 82 us (0.40)
  Pallas kernels: 0 us -> 73.8 us
  local copies, waits for them, and re-layouts: 64.6 us -> 5.7 us
  other arithmetic: 59.9 us -> 2.19 us
  waiting for transfers between devices: 44.5 us -> 0 us
  starting transfers between devices: 22.8 us -> 0 us
  matrix products: 13.8 us -> 0 us
    pallas_call x0 -> x1, Pallas kernels: none -> 73.8 us  [coupled(): pl.pallas_call(functools.partial(kernel, cap, parts), out_shape=[jax.Shap...]
    all_to_all x2 -> x0, waiting for transfers between devices: 44.4 us -> none  [the longest x1 30.3 us: on_device(): lax.all_to_all(outgoing, ('bins', 'tiles'), split_axis=1, concat_axis=1,...]
    gt x2 -> x0, other arithmetic: 26.9 us -> none  [the longest x1 26.8 us: advance(): up_x = jnp.where(cxb > 0, west, east)]
    gather x5 -> x0, local copies, waits for them, and re-layouts: 20.6 us -> none  [the longest x1 9.21 us: on_device(): picked = jnp.take(flat, jnp.maximum(listing, 0), axis=1)]
    all_to_all x2 -> x0, starting transfers between devices: 18.5 us -> none  [the longest x1 13.8 us: on_device(): lax.all_to_all(picked, ('bins', 'tiles'), split_axis=1, concat_axis=1, ti...]
    reshape x2 -> x0, local copies, waits for them, and re-layouts: 15.9 us -> none  [the longest x1 8 us: on_device(): quad3_b = quad_b.reshape(groups, group_bins, all_bins)]
    convert_element_type x3 -> x0, other arithmetic: 15.8 us -> none  [the longest x1 10.1 us: on_device(): sent_here = prop.astype(jnp.bfloat16)]
    dot_general x2 -> x0, matrix products: 13.8 us -> none  [the longest x1 7.35 us: on_device(): lax.dot_general(quad3_a, received, dims, preferred_element_type=jnp.float32)]
  transfers between devices with their start and end apart: 4 -> 0, of which waited for: 2 -> 0; matrix products, arithmetic and copies ran while one was open for 28% -> 0% of each run, Pallas kernels for 0% -> 0%
where the time goes in v1:
time: 82 us; the launch traced here: 81.7 us
  Pallas kernels  73.8 us (90%)
  local copies, waits for them, and re-layouts  5.7 us (7%)
  other arithmetic  2.19 us (3%)
    pallas_call x1, Pallas kernels, coupled(): pl.pallas_call(functools.partial(kernel, cap, parts), out_shape=[jax.Shap...  73.8 us
    unnamed x1, local copies, waits for them, and re-layouts  4.12 us

profile of v1, /device:TPU:0, one launch (start us, length us, event | category | flops | bytes accessed | tf_op | source)
XLA Modules:
  0.0 81.7 jit_solution(274563383618844734)
XLA Ops:
  0.0 0.7 broadcast_multiply_fusion.3
  0.7 0.7 broadcast_multiply_fusion.2
  1.4 0.8 broadcast_multiply_fusion.1
  2.2 0.1 mul.53
  2.3 0.1 mul.56
  2.5 0.3 copy.15
  2.8 1.0 %pad.4.coef = f32[1808,4]{1,0:T(8,128)} pad(f32[1800,4]{1,0:T(8,128)S(1)} %copy.15, f32[]{:T(128)} %constant.8.clone.1), padding=0_8x0_0 | pad | bytes 57732 | tf_op jit(solution)/shard_map/jit(_pad)/pad | solution.py:518
  3.8 73.8 %coupled512.1 = (f32[450,8,256]{2,1,0:T(8,128)}, f32[8,128]{1,0:T(8,128)}) custom-call(f32[450,8,256]{2,1,0:T(8,128)} %spec.1, bf16[1800,1800]{1,0:T(8,128)(2,1)} %quad_a.1, bf16[1800,1800]{1,0:T(8,128)(2,1)} %quad_b.1, f32[1808,4]{1,0:T(8,128)} %pad.4.coef, f32[1,512]{1,0:T(1,128)} %wind.1, s32[8,256]{1,0:T(8,128)} %slot.1), custom_call_target="tpu_custom_call" | custom-call | tf_op jit(solution)/shard_map/coupled512/pallas_call | solution.py:457
  77.6 4.1 %copy.17 = f32[450,8,256]{2,1,0:T(8,128)} copy(f32[450,8,256]{2,1,0:T(8,128)} %get-tuple-element.6) | data formatting | bytes 7372800
  (3 shorter events, 0.1 us)

commit v2 on v1

--- a/solution.py
+++ b/solution.py
@@ -3,7 +3,6 @@
 
 import jax
 import jax.numpy as jnp
-import numpy as np
 from jax import lax
 from jax.experimental import pallas as pl
 from jax.experimental.pallas import tpu as pltpu
@@ -33,7 +32,9 @@
     spec,
     quad_a,
     quad_b,
-    coef,
+    speed,
+    growth,
+    dissip,
     wind,
     slot,
     out,
@@ -44,6 +45,8 @@
     sea,
     place,
     onehot,
+    rates,
+    coef,
     halo_out,
     halo_in,
     prop,
@@ -93,9 +96,6 @@
         load.start()
     load_a = pltpu.make_async_copy(quad_a, qa, load_sem.at[2])
     load_b = pltpu.make_async_copy(quad_b, qb, load_sem.at[3])
-    load_a.start()
-    load_b.start()
-
     barrier = pltpu.get_barrier_semaphore()
     peers = [(lax.rem(z + i, 4), t) for i in (1, 2, 3)]
     peers += [(z, lax.rem(t + 1, TILES)), (z, lax.rem(t + TILES - 1, TILES))]
@@ -135,17 +135,119 @@
         for h, at in enumerate(strip(i, r)):
             flat[at, :] = value[:, 128 * h : 128 * h + 128]
 
+    def both(k, i):
+        one = coef[k, pl.ds(pl.multiple_of(64 + i * SUB, SUB), SUB), :]
+        return jnp.concatenate([one, one], axis=1)
+
+    mark = lax.broadcasted_iota(jnp.int32, (1, 128), 1)
+    for p in range(TILES):
+        row = wind[:, 128 * (p // 8) : 128 * (p // 8) + 128]
+        if p % 8:
+            row = pltpu.roll(row, 128 - MOST * (p % 8), 1)
+        wp[p // 8, (p // 2) % 4, p % 2] = jnp.where(mark == MOST, fullest, row)
+    wz[z] = wp[...]
+
+    def wind_copy(k, src, dst, there):
+        return pltpu.make_async_remote_copy(
+            src_ref=src,
+            dst_ref=dst,
+            send_sem=wind_send.at[k],
+            recv_sem=wind_recv.at[k],
+            device_id=there,
+            device_id_type=MESH,
+        )
+
+    def wind_z():
+        return [wind_copy(i, wp, wz.at[z], (lax.rem(z + 1 + i, 4), t)) for i in range(3)]
+
+    def wind_y():
+        return [
+            wind_copy(3 + i, wz.at[:, p], wy.at[ty], (z, p * 8 + lax.rem(t, 8)))
+            for i, p in enumerate(ypeers)
+        ]
+
+    def wind_x():
+        return [
+            wind_copy(6 + i, wy.at[:, :, p], wx.at[tx], (z, ty * 8 + p * 2 + tc))
+            for i, p in enumerate(xpeers)
+        ]
+
+    def wind_c():
+        return [wind_copy(9, wx.at[:, :, :, 1 - tc], wc.at[tc], (z, t + 1 - 2 * tc))]
+
+    def wind_next(stage):
+        if stage == 0:
+            for copy in wind_z():
+                copy.start()
+        if stage == 1:
+            for copy in wind_z():
+                copy.wait()
+            wy[ty] = wz[:, ty]
+            for copy in wind_y():
+                copy.start()
+        if stage == 2:
+            for copy in wind_y():
+                copy.wait()
+            wx[tx] = wy[:, :, tx]
+            for copy in wind_x():
+                copy.start()
+        if stage == 3:
+            for copy in wind_x():
+                copy.wait()
+            wc[tc] = wx[:, :, :, tc]
+            for copy in wind_c():
+                copy.start()
+        if stage == 4:
+            for copy in wind_c():
+                copy.wait()
+            for i in range(128):
+                table[i : i + 1, :] = wc[i // 64, (i // 16) % 4, (i // 4) % 4, i % 4]
+
+    odd_start = z % 2
+    first = (7 * z) // 2
+    rates[...] = jnp.zeros((8, 1920), F32)
+    rates[0:1, 0:BINS] = 0.25 * growth[...]
+    rates[1:2, 0:BINS] = 0.25 * dissip[...]
+    rates[2:3, 0:50] = speed[...]
+    speeds = jnp.broadcast_to(rates[2:3, 0:128], (8, 128))
+    speed_high = speeds.astype(BF16)
+    speed_mid = (speeds - speed_high.astype(F32)).astype(BF16)
+    speed_low = (speeds - speed_high.astype(F32) - speed_mid.astype(F32)).astype(BF16)
+    for j in range(5):
+        block = first + j
+        bins = block * 128 + lax.broadcasted_iota(jnp.int32, (128, 128), 1)
+        pick = jnp.where(lax.broadcasted_iota(jnp.int32, (128, 128), 0) == bins % 50, 1.0, 0.0).astype(BF16)
+        rate = sum(
+            jnp.dot(part, pick, preferred_element_type=F32) for part in (speed_high, speed_mid, speed_low)
+        )
+        theta = ((bins[0:8] // 50).astype(F32) + 0.5) * (2.0 * math.pi / 36)
+        cosine = jnp.abs(jnp.cos(theta))
+        sine = jnp.abs(jnp.sin(theta))
+        total = cosine + sine
+        at = pl.ds(pl.multiple_of(block * 128, 128), 128)
+        lines = [
+            (rate * cosine / total)[0:1],
+            (rate * sine / total)[0:1],
+            rates[0:1, at],
+            rates[1:2, at],
+        ]
+        for k, line in enumerate(lines):
+            there = pl.ds(pl.multiple_of(128 * j + 64 - 64 * odd_start, 8), 128)
+            coef[k, there, :] = jnp.broadcast_to(line, (128, 128)).T
+
     for load in load_x:
         load.wait()
+    load_a.start()
+    load_b.start()
     edge = 7 * west
     edge_sea = sea[pl.ds(edge, 1), :]
 
     def halo_step(i, carry):
         v = take(i, edge)
-        halo_out[pl.ds(pl.multiple_of(i * SUB, SUB), SUB), :] = v * edge_sea
+        halo_out[pl.ds(pl.multiple_of(i * SUB, SUB), SUB), :] = (v * edge_sea).astype(BF16)
         return carry
 
-    lax.fori_loop(0, count, halo_step, 0)
+    lax.fori_loop(0, count, halo_step, 0, unroll=4)
     pl.semaphore_wait(barrier, len(peers))
     halo = pltpu.make_async_remote_copy(
         src_ref=halo_out,
@@ -156,6 +258,7 @@
         device_id_type=MESH,
     )
     halo.start()
+    wind_next(0)
     outer = (1 - west) * (TILES - 1)
     halo_there = (t != outer).astype(F32)
 
@@ -179,10 +282,9 @@
             f1 = take(i, r0 + 1) * sea1
             fu = take(i, ru) * seau
             if edged:
-                fu = jnp.where(at_edge, halo_in[here, :] * halo_there, fu)
-            consts = coef[pl.ds(pl.multiple_of(z * STEP + i * SUB, SUB), SUB), :]
-            cx = consts[:, 0:1]
-            cy = consts[:, 1:2]
+                fu = jnp.where(at_edge, halo_in[here, :].astype(F32) * halo_there, fu)
+            cx = both(0, i)
+            cy = both(1, i)
             up0 = jnp.where(from_west, fu, f1)
             up1 = jnp.where(from_west, f0, fu)
             y0 = jnp.where(wall, 0.0, pltpu.roll(f0, shift, 1))
@@ -195,18 +297,18 @@
             sent[here, COLS:CELLS] = p1.astype(BF16)
             return carry
 
-        lax.fori_loop(0, count, step, 0)
+        lax.fori_loop(0, count, step, 0, unroll=4)
         rank = lax.broadcasted_iota(jnp.int32, (cap, COLS), 0).astype(F32)
         onehot[g, :, 0:COLS] = jnp.where(rank == place[pl.ds(r0, 1), :], 1.0, 0.0).astype(BF16)
         onehot[g, :, COLS:CELLS] = jnp.where(rank == place[pl.ds(r0 + 1, 1), :], 1.0, 0.0).astype(BF16)
         return lax.dot_general(sent[...], onehot[g], NT, preferred_element_type=F32).astype(BF16)
 
     late = z // 3
+    early = (3 - z) // 3
     order = [
         1 + lax.rem(z, 2),
         2 * (1 - (z + 2) // 3) + late,
         3 * (1 - late),
-        z,
     ]
 
     starts = [sum(parts[:i]) for i in range(len(parts))]
@@ -221,82 +323,27 @@
             device_id_type=MESH,
         )
 
-    for i in range(3):
-        if i == 2:
-            halo.wait()
-        ahead[i] = propagate(order[i], i == 2)
-        forward(i, 0).start()
-    for c in range(1, len(parts)):
-        for i in range(3):
+    for i in range(2):
+        ahead[i] = propagate(order[i], False)
+        for c in range(len(parts)):
             forward(i, c).start()
-    held[z, 0:WIN, :] = propagate(z, True)
-
-    mark = lax.broadcasted_iota(jnp.int32, (1, 128), 1)
-    for p in range(TILES):
-        row = wind[:, 128 * (p // 8) : 128 * (p // 8) + 128]
-        if p % 8:
-            row = pltpu.roll(row, 128 - MOST * (p % 8), 1)
-        wp[p // 8, (p // 2) % 4, p % 2] = jnp.where(mark == MOST, fullest, row)
-    wy[ty] = wp[ty]
-
-    def wind_copy(k, src, dst, there):
-        return pltpu.make_async_remote_copy(
-            src_ref=src,
-            dst_ref=dst,
-            send_sem=wind_send.at[k],
-            recv_sem=wind_recv.at[k],
-            device_id=there,
-            device_id_type=MESH,
-        )
-
-    def wind_y():
-        return [
-            wind_copy(i, wp.at[p], wy.at[ty], (z, p * 8 + lax.rem(t, 8))) for i, p in enumerate(ypeers)
-        ]
-
-    def wind_x():
-        return [
-            wind_copy(3 + i, wy.at[:, p], wx.at[tx], (z, ty * 8 + p * 2 + tc)) for i, p in enumerate(xpeers)
-        ]
-
-    def wind_c():
-        return [wind_copy(6, wx.at[:, :, 1 - tc], wc.at[tc], (z, t + 1 - 2 * tc))]
-
-    def wind_z():
-        return [
-            wind_copy(7 + i, wc, wz.at[z], (lax.rem(z + 1 + i, 4), t)) for i in range(3)
-        ]
-
-    def wind_next(stage):
-        if stage == 0:
-            for copy in wind_y():
-                copy.start()
-        if stage == 1:
-            for copy in wind_y():
-                copy.wait()
-            wx[tx] = wy[:, tx]
-            for copy in wind_x():
-                copy.start()
-        if stage == 2:
-            for copy in wind_x():
-                copy.wait()
-            wc[tc] = wx[:, :, tc]
-            for copy in wind_c():
-                copy.start()
-        if stage == 3:
-            for copy in wind_c():
-                copy.wait()
-            wz[z] = wc[...]
-            for copy in wind_z():
-                copy.start()
-        if stage == 4:
-            for copy in wind_z():
-                copy.wait()
-            for i in range(128):
-                table[i : i + 1, :] = wz[i // 32, (i // 16) % 2, (i // 4) % 4, i % 4]
-
-    wind_next(0)
-
+
+    def keep(mine, block):
+        @pl.when(mine)
+        def _():
+            held[z, 0:WIN, :] = block
+
+        @pl.when(jnp.logical_not(mine))
+        def _():
+            ahead[2] = block
+
+    keep(z > 0, propagate(z + 3 * early, False))
+    wind_next(1)
+    halo.wait()
+    keep(z == 0, propagate(order[2] * (1 - early), True))
+    for c in range(len(parts)):
+        forward(2, c).start()
+    wind_next(2)
     load_a.wait()
     load_b.wait()
 
@@ -337,7 +384,8 @@
         at = pl.ds(starts[c], n)
         for i in range(3):
             landing(c, i).wait_recv()
-        wind_next(1 + c)
+        if c < 2:
+            wind_next(3 + c)
         ones = jnp.ones((SUB, 512), BF16)
         mean = jnp.zeros((SUB, n), F32)
         for s in range(GROUPS):
@@ -376,8 +424,6 @@
         for i in range(3):
             returning(i, c).start()
 
-    for stage in range(1 + len(parts), 5):
-        wind_next(stage)
     most[...] = jnp.broadcast_to(jnp.max(table[:, MOST : MOST + 1]), (8, 128))
 
     wide = table[...]
@@ -394,7 +440,7 @@
     def wind_row(r):
         cells = slot[pl.ds(r, 1), :]
         shard = cells // MOST
-        line = (shard // 32) * 32 + (shard % 2) * 16 + ((shard // 2) % 4) * 4 + (shard // 8) % 4
+        line = (shard % 2) * 64 + ((shard // 2) % 4) * 16 + ((shard // 8) % 4) * 4 + shard // 32
         pick = lax.broadcasted_iota(jnp.int32, (128, COLS), 0) == line
         pick = jnp.where(pick, 1.0, 0.0).astype(BF16)
         found = sum(jnp.dot(w, pick, preferred_element_type=F32) for w in tables)
@@ -412,9 +458,8 @@
 
         def step(i, carry):
             here = pl.ds(pl.multiple_of(i * SUB, SUB), SUB)
-            consts = coef[pl.ds(pl.multiple_of(z * STEP + i * SUB, SUB), SUB), :]
-            grow = consts[:, 2:3]
-            damp = consts[:, 3:4]
+            grow = both(2, i)
+            damp = both(3, i)
             p0 = prop[g, here, 0:COLS]
             p1 = prop[g, here, COLS:CELLS]
             s0 = p0.astype(BF16).astype(F32)
@@ -425,7 +470,7 @@
             put(i, r0 + 1, e1)
             return carry
 
-        lax.fori_loop(0, count, step, 0)
+        lax.fori_loop(0, count, step, 0, unroll=4)
 
     finish(z, back)
     for i in range(3):
@@ -448,7 +493,7 @@
         store.wait()
 
 
-def coupled(cap, parts, cid, spectrum, quad_a, quad_b, coef, wind, slot):
+def coupled(cap, parts, cid, spectrum, speed, quad_a, quad_b, growth, dissip, wind, slot):
     vmem = pl.BlockSpec(memory_space=pltpu.VMEM)
     hbm = pl.BlockSpec(memory_space=pl.ANY)
     n = len(parts)
@@ -460,7 +505,7 @@
             jax.ShapeDtypeStruct(spectrum.shape, F32),
             jax.ShapeDtypeStruct((8, 128), F32),
         ],
-        in_specs=[hbm, hbm, hbm, vmem, vmem, vmem],
+        in_specs=[hbm, hbm, hbm, vmem, vmem, vmem, vmem, vmem],
         out_specs=[hbm, vmem],
         scratch_shapes=[
             pltpu.VMEM((2, WIN, ROWS, 128), F32),
@@ -469,8 +514,10 @@
             pltpu.VMEM((ROWS, COLS), F32),
             pltpu.VMEM((ROWS, COLS), F32),
             pltpu.VMEM((GROUPS, cap, CELLS), BF16),
-            pltpu.VMEM((WIN, COLS), F32),
-            pltpu.VMEM((WIN, COLS), F32),
+            pltpu.VMEM((8, 1920), F32),
+            pltpu.VMEM((4, 704, 128), F32),
+            pltpu.VMEM((WIN, COLS), BF16),
+            pltpu.VMEM((WIN, COLS), BF16),
             pltpu.VMEM((GROUPS, WIN, CELLS), F32),
             pltpu.VMEM((WIN, CELLS), BF16),
             pltpu.VMEM((3, WIN, cap), BF16),
@@ -482,10 +529,10 @@
             pltpu.VMEM((GROUPS, WIN, cap), BF16),
             pltpu.VMEM((WIN, CELLS), F32),
             pltpu.VMEM((4, 4, 2, 1, 128), F32),
-            pltpu.VMEM((4, 4, 2, 1, 128), F32),
-            pltpu.VMEM((4, 4, 2, 1, 128), F32),
-            pltpu.VMEM((2, 4, 4, 1, 128), F32),
-            pltpu.VMEM((4, 2, 4, 4, 1, 128), F32),
+            pltpu.VMEM((4, 4, 4, 2, 1, 128), F32),
+            pltpu.VMEM((4, 4, 4, 2, 1, 128), F32),
+            pltpu.VMEM((2, 4, 4, 4, 1, 128), F32),
+            pltpu.VMEM((4, 4, 4, 2, 1, 128), F32),
             pltpu.VMEM((128, 128), F32),
             dma((4,)),
             dma((2,)),
@@ -500,24 +547,17 @@
             collective_id=cid, has_side_effects=True, vmem_limit_bytes=56 << 20
         ),
         name="coupled%d" % cap,
-    )(spectrum, quad_a, quad_b, coef, wind, slot)
-
-
-def directions():
-    theta = (np.arange(36) + 0.5) * (2.0 * math.pi / 36)
-    cosine = np.abs(np.cos(theta))
-    sine = np.abs(np.sin(theta))
-    return cosine / (cosine + sine), sine / (cosine + sine)
+    )(spectrum, quad_a, quad_b, speed[None], growth[None], dissip[None], wind, slot)
 
 
 def on_device(spectrum, speed, quad_a, quad_b, growth, dissip, wind, cell_slot):
-    along, across = directions()
-    cx = (jnp.asarray(along, F32)[:, None] * speed[None, :]).reshape(BINS)
-    cy = (jnp.asarray(across, F32)[:, None] * speed[None, :]).reshape(BINS)
-    coef = jnp.stack([cx, cy, 0.25 * growth, 0.25 * dissip], axis=1)
-    coef = jnp.pad(coef, ((0, 8), (0, 0)))
-    out, most = coupled(512, (256, 256), 0, spectrum, quad_a, quad_b, coef, wind, cell_slot)
-    return out
+    inputs = (spectrum, speed, quad_a, quad_b, growth, dissip, wind, cell_slot)
+    out, most = coupled(384, (128, 128, 128), 0, *inputs)
+    return lax.cond(
+        most[0, 0] > 384.0,
+        lambda: coupled(CELLS, (128, 128, 128, 128), 1, *inputs)[0],
+        lambda: out,
+    )
 
 
 def solution(mesh):

time: 82 us -> 57.7 us (0.70)
  the two profiles are of different devices: /device:TPU:0 before, /device:TPU:88 now
where the time goes in v2:
time: 57.7 us; the launch traced here: 57.4 us
  Pallas kernels  48.5 us (84%)
  local copies, waits for them, and re-layouts  7.93 us (14%)
  between operations  0.74 us (1%)
    pallas_call x1, Pallas kernels, coupled(): pl.pallas_call(functools.partial(kernel, cap, parts), out_shape=[jax.Shap...  48.5 us
    unnamed x13, local copies, waits for them, and re-layouts  4.15 us
    broadcast_in_dim x1, local copies, waits for them, and re-layouts, coupled(): growth[None]  1.3 us
    broadcast_in_dim x1, local copies, waits for them, and re-layouts, coupled(): dissip[None]  1.29 us
    slice x1, local copies, waits for them, and re-layouts, on_device(): most[0, 0] > 384.0  1.19 us

profile of v2, /device:TPU:88, one launch (start us, length us, event | category | flops | bytes accessed | tf_op | source)
XLA Modules:
  0.0 57.4 jit_solution(9157520790200534953)
XLA Ops:
  0.0 1.3 %broadcast_in_dim.19.growth = f32[1,1800]{1,0:T(1,128)} reshape(f32[1800]{0:T(1024)} %param.14) | data formatting | bytes 14400 | tf_op jit(solution)/shard_map/broadcast_in_dim | solution.py:550
  1.3 1.3 %broadcast_in_dim.20.dissip = f32[1,1800]{1,0:T(1,128)} reshape(f32[1800]{0:T(1024)} %param.15) | data formatting | bytes 14400 | tf_op jit(solution)/shard_map/broadcast_in_dim | solution.py:550
  2.6 0.0 copy-start
  2.6 0.0 copy-start.1
  2.6 0.0 copy-start.2
  2.6 0.0 copy-start.3
  2.6 0.0 copy-start.4
  2.6 0.0 copy-start.5
  2.6 48.5 %coupled384.1 = (f32[450,8,256]{2,1,0:T(8,128)}, f32[8,128]{1,0:T(8,128)}) custom-call(f32[450,8,256]{2,1,0:T(8,128)} %spec.1, bf16[1800,1800]{1,0:T(8,128)(2,1)} %quad_a.1, bf16[1800,1800]{1,0:T(8,128)(2,1)} %quad_b.1, f32[1,50]{1,0:T(1,128)} %bitcast.3, f32[1,1800]{1,0:T(1,128)} %broadcast_in_dim.19.growth, f32[1,1800]{1,0:T(1,128)} %broadcast_in_dim.20.dissip, ...), custom_call_target="tpu_custom_call" | custom-call | tf_op jit(solution)/shard_map/coupled384/pallas_call | solution.py:502
  51.1 1.2 %slice.3 = f32[1,1]{1,0:T(1,128)} slice(f32[8,128]{1,0:T(8,128)} %get-tuple-element.36), slice={[0:1], [0:1]} | slice | bytes 8 | tf_op jit(solution)/shard_map/slice | solution.py:557
  53.0 0.0 copy-done
  53.0 0.0 copy-done.1
  53.0 0.0 copy-done.2
  53.0 0.0 copy-done.3
  53.0 0.0 copy-done.4
  53.0 0.0 copy-done.5
  53.0 0.2 conditional.1
  53.3 4.1 %copy.14 = f32[450,8,256]{2,1,0:T(8,128)} copy(f32[450,8,256]{2,1,0:T(8,128)} %get-tuple-element.38) | data formatting | bytes 7372800
Async XLA Ops:
  2.6 50.4 %copy-start = (bf16[1800,1800]{1,0:T(8,128)(2,1)S(1)}, bf16[1800,1800]{1,0:T(8,128)(2,1)}, u32[]{:S(2)}) copy-start(bf16[1800,1800]{1,0:T(8,128)(2,1)} %quad_a.1) | copy-start | bytes 19440004
  2.6 50.4 %copy-start.1 = (s32[8,256]{1,0:T(8,128)S(1)}, s32[8,256]{1,0:T(8,128)}, u32[]{:S(2)}) copy-start(s32[8,256]{1,0:T(8,128)} %slot.1) | copy-start | bytes 24580
  2.6 50.4 %copy-start.2 = (f32[1800]{0:T(1024)S(1)}, f32[1800]{0:T(1024)}, u32[]{:S(2)}) copy-start(f32[1800]{0:T(1024)} %param.14) | copy-start | bytes 21604
  2.6 50.4 %copy-start.3 = (f32[1800]{0:T(1024)S(1)}, f32[1800]{0:T(1024)}, u32[]{:S(2)}) copy-start(f32[1800]{0:T(1024)} %param.15) | copy-start | bytes 21604
  2.6 50.4 %copy-start.4 = (f32[1,512]{1,0:T(1,128)S(1)}, f32[1,512]{1,0:T(1,128)}, u32[]{:S(2)}) copy-start(f32[1,512]{1,0:T(1,128)} %wind.1) | copy-start | bytes 6148
  2.6 50.4 %copy-start.5 = (f32[50]{0:T(128)S(1)}, f32[50]{0:T(128)}, u32[]{:S(2)}) copy-start(f32[50]{0:T(128)} %param.11) | copy-start | bytes 604

commit v3 on v2

--- a/solution.py
+++ b/solution.py
@@ -206,9 +206,9 @@
     odd_start = z % 2
     first = (7 * z) // 2
     rates[...] = jnp.zeros((8, 1920), F32)
-    rates[0:1, 0:BINS] = 0.25 * growth[...]
-    rates[1:2, 0:BINS] = 0.25 * dissip[...]
-    rates[2:3, 0:50] = speed[...]
+    rates[0:1, 0:BINS] = 0.25 * growth[...][None]
+    rates[1:2, 0:BINS] = 0.25 * dissip[...][None]
+    rates[2:3, 0:50] = speed[...][None]
     speeds = jnp.broadcast_to(rates[2:3, 0:128], (8, 128))
     speed_high = speeds.astype(BF16)
     speed_mid = (speeds - speed_high.astype(F32)).astype(BF16)
@@ -424,7 +424,7 @@
         for i in range(3):
             returning(i, c).start()
 
-    most[...] = jnp.broadcast_to(jnp.max(table[:, MOST : MOST + 1]), (8, 128))
+    most[0] = (jnp.max(table[:, MOST : MOST + 1]) > cap).astype(jnp.int32)
 
     wide = table[...]
     w_high = wide.astype(BF16)
@@ -477,20 +477,12 @@
         for c in range(len(parts)):
             homing(c, i).wait_recv()
         finish(lax.rem(z + i + 1, 4), got)
-    stores = [
-        pltpu.make_async_copy(
-            field.at[h, pl.ds(2 * z, OWN)], out.at[:, :, pl.ds(128 * h, 128)], load_sem.at[h]
-        )
-        for h in range(2)
-    ]
-    for store in stores:
-        store.start()
+    for h in range(2):
+        out[:, :, 128 * h : 128 * h + 128] = field[h, pl.ds(2 * z, OWN)]
     for i in range(3):
         for c in range(len(parts)):
             forward(i, c).wait_send()
             returning(i, c).wait_send()
-    for store in stores:
-        store.wait()
 
 
 def coupled(cap, parts, cid, spectrum, speed, quad_a, quad_b, growth, dissip, wind, slot):
@@ -502,11 +494,11 @@
     return pl.pallas_call(
         functools.partial(kernel, cap, parts),
         out_shape=[
-            jax.ShapeDtypeStruct(spectrum.shape, F32),
-            jax.ShapeDtypeStruct((8, 128), F32),
+            pltpu.VMEM(spectrum.shape, F32),
+            jax.ShapeDtypeStruct((1,), jnp.int32),
         ],
         in_specs=[hbm, hbm, hbm, vmem, vmem, vmem, vmem, vmem],
-        out_specs=[hbm, vmem],
+        out_specs=[vmem, pl.BlockSpec(memory_space=pltpu.SMEM)],
         scratch_shapes=[
             pltpu.VMEM((2, WIN, ROWS, 128), F32),
             pltpu.VMEM((BINS, BINS), BF16),
@@ -547,17 +539,18 @@
             collective_id=cid, has_side_effects=True, vmem_limit_bytes=56 << 20
         ),
         name="coupled%d" % cap,
-    )(spectrum, quad_a, quad_b, speed[None], growth[None], dissip[None], wind, slot)
+    )(spectrum, quad_a, quad_b, speed, growth, dissip, wind, slot)
 
 
 def on_device(spectrum, speed, quad_a, quad_b, growth, dissip, wind, cell_slot):
     inputs = (spectrum, speed, quad_a, quad_b, growth, dissip, wind, cell_slot)
     out, most = coupled(384, (128, 128, 128), 0, *inputs)
-    return lax.cond(
-        most[0, 0] > 384.0,
+    out = lax.cond(
+        most[0] != 0,
         lambda: coupled(CELLS, (128, 128, 128, 128), 1, *inputs)[0],
         lambda: out,
     )
+    return out
 
 
 def solution(mesh):

time: 57.7 us -> 49.8 us (0.86)
  local copies, waits for them, and re-layouts: 7.93 us -> 1.87 us
  Pallas kernels: 48.5 us -> 46.9 us
    broadcast_in_dim x2 -> x0, local copies, waits for them, and re-layouts: 2.59 us -> none  [the longest x1 1.3 us: coupled(): growth[None]]
    unnamed x13, local copies, waits for them, and re-layouts: 4.15 us -> 1.87 us
    pallas_call x1, Pallas kernels: 48.5 us -> 46.9 us  [coupled(): pl.pallas_call(functools.partial(kernel, cap, parts), out_shape=[pltpu.VM...]
    slice x1 -> x0, local copies, waits for them, and re-layouts: 1.19 us -> none  [on_device(): most[0, 0] > 384.0]
where the time goes in v3:
time: 49.8 us; the launch traced here: 49.7 us
  Pallas kernels  46.9 us (94%)
  local copies, waits for them, and re-layouts  1.87 us (4%)
  between operations  0.72 us (1%)
    pallas_call x1, Pallas kernels, coupled(): pl.pallas_call(functools.partial(kernel, cap, parts), out_shape=[pltpu.VM...  46.9 us
    unnamed x13, local copies, waits for them, and re-layouts  1.87 us

profile of v3, /device:TPU:88, one launch (start us, length us, event | category | flops | bytes accessed | tf_op | source)
XLA Modules:
  0.0 49.7 jit_solution(921069862970471550)
XLA Ops:
  0.0 0.0 copy-start
  0.0 0.0 copy-start.1
  0.0 0.0 copy-start.2
  0.0 0.0 copy-start.3
  0.0 0.0 copy-start.4
  0.0 0.0 copy-start.5
  0.0 46.9 %coupled384.1 = (f32[450,8,256]{2,1,0:T(8,128)S(1)}, s32[1]{0:T(128)}) custom-call(f32[450,8,256]{2,1,0:T(8,128)} %spec.1, bf16[1800,1800]{1,0:T(8,128)(2,1)} %quad_a.1, bf16[1800,1800]{1,0:T(8,128)(2,1)} %quad_b.1, f32[50]{0:T(128)} %speed.1, f32[1800]{0:T(1024)} %growth.1, f32[1800]{0:T(1024)} %dissip.1, f32[1,512]{1,0:T(1,128)} %wind.1, s32[8,256]{1,0:T(8,128)} %slot.1), custom_call_target="tpu_custom_call" | custom-call | tf_op jit(solution)/shard_map/coupled384/pallas_call | solution.py:494
  47.6 0.0 copy-done
  47.6 0.0 copy-done.1
  47.6 0.0 copy-done.2
  47.6 0.0 copy-done.3
  47.6 0.0 copy-done.4
  47.6 0.0 copy-done.5
  47.6 0.2 conditional.1
  47.8 1.8 %copy.14 = f32[450,8,256]{2,1,0:T(8,128)} copy(f32[450,8,256]{2,1,0:T(8,128)S(1)} %get-tuple-element.38) | data formatting | bytes 7372800
Async XLA Ops:
  0.0 47.6 %copy-start = (f32[450,8,256]{2,1,0:T(8,128)S(1)}, f32[450,8,256]{2,1,0:T(8,128)}, u32[]{:S(2)}) copy-start(f32[450,8,256]{2,1,0:T(8,128)} %spec.1) | copy-start | bytes 11059204
  0.0 47.6 %copy-start.1 = (f32[1800]{0:T(1024)S(1)}, f32[1800]{0:T(1024)}, u32[]{:S(2)}) copy-start(f32[1800]{0:T(1024)} %growth.1) | copy-start | bytes 21604
  0.0 47.6 %copy-start.2 = (f32[1800]{0:T(1024)S(1)}, f32[1800]{0:T(1024)}, u32[]{:S(2)}) copy-start(f32[1800]{0:T(1024)} %dissip.1) | copy-start | bytes 21604
  0.0 47.6 %copy-start.3 = (s32[8,256]{1,0:T(8,128)S(1)}, s32[8,256]{1,0:T(8,128)}, u32[]{:S(2)}) copy-start(s32[8,256]{1,0:T(8,128)} %slot.1) | copy-start | bytes 24580
  0.0 47.6 %copy-start.4 = (f32[1,512]{1,0:T(1,128)S(1)}, f32[1,512]{1,0:T(1,128)}, u32[]{:S(2)}) copy-start(f32[1,512]{1,0:T(1,128)} %wind.1) | copy-start | bytes 6148
  0.0 47.6 %copy-start.5 = (f32[50]{0:T(128)S(1)}, f32[50]{0:T(128)}, u32[]{:S(2)}) copy-start(f32[50]{0:T(128)} %speed.1) | copy-start | bytes 604

commit v4 on v3

--- a/solution.py
+++ b/solution.py
@@ -65,6 +65,7 @@
     wc,
     wz,
     table,
+    winds,
     load_sem,
     halo_sem,
     fwd_send,
@@ -138,14 +139,6 @@
     def both(k, i):
         one = coef[k, pl.ds(pl.multiple_of(64 + i * SUB, SUB), SUB), :]
         return jnp.concatenate([one, one], axis=1)
-
-    mark = lax.broadcasted_iota(jnp.int32, (1, 128), 1)
-    for p in range(TILES):
-        row = wind[:, 128 * (p // 8) : 128 * (p // 8) + 128]
-        if p % 8:
-            row = pltpu.roll(row, 128 - MOST * (p % 8), 1)
-        wp[p // 8, (p // 2) % 4, p % 2] = jnp.where(mark == MOST, fullest, row)
-    wz[z] = wp[...]
 
     def wind_copy(k, src, dst, there):
         return pltpu.make_async_remote_copy(
@@ -213,6 +206,11 @@
     speed_high = speeds.astype(BF16)
     speed_mid = (speeds - speed_high.astype(F32)).astype(BF16)
     speed_low = (speeds - speed_high.astype(F32) - speed_mid.astype(F32)).astype(BF16)
+
+    def columns(k, j, line):
+        there = pl.ds(pl.multiple_of(128 * j + 64 - 64 * odd_start, 8), 128)
+        coef[k, there, :] = jnp.broadcast_to(line, (128, 128)).T
+
     for j in range(5):
         block = first + j
         bins = block * 128 + lax.broadcasted_iota(jnp.int32, (128, 128), 1)
@@ -224,16 +222,8 @@
         cosine = jnp.abs(jnp.cos(theta))
         sine = jnp.abs(jnp.sin(theta))
         total = cosine + sine
-        at = pl.ds(pl.multiple_of(block * 128, 128), 128)
-        lines = [
-            (rate * cosine / total)[0:1],
-            (rate * sine / total)[0:1],
-            rates[0:1, at],
-            rates[1:2, at],
-        ]
-        for k, line in enumerate(lines):
-            there = pl.ds(pl.multiple_of(128 * j + 64 - 64 * odd_start, 8), 128)
-            coef[k, there, :] = jnp.broadcast_to(line, (128, 128)).T
+        columns(0, j, (rate * cosine / total)[0:1])
+        columns(1, j, (rate * sine / total)[0:1])
 
     for load in load_x:
         load.wait()
@@ -258,6 +248,13 @@
         device_id_type=MESH,
     )
     halo.start()
+    mark = lax.broadcasted_iota(jnp.int32, (1, 128), 1)
+    for p in range(TILES):
+        row = wind[:, 128 * (p // 8) : 128 * (p // 8) + 128]
+        if p % 8:
+            row = pltpu.roll(row, 128 - MOST * (p % 8), 1)
+        wp[p // 8, (p // 2) % 4, p % 2] = jnp.where(mark == MOST, fullest, row)
+    wz[z] = wp[...]
     wind_next(0)
     outer = (1 - west) * (TILES - 1)
     halo_there = (t != outer).astype(F32)
@@ -338,14 +335,18 @@
             ahead[2] = block
 
     keep(z > 0, propagate(z + 3 * early, False))
-    wind_next(1)
     halo.wait()
     keep(z == 0, propagate(order[2] * (1 - early), True))
     for c in range(len(parts)):
         forward(2, c).start()
-    wind_next(2)
+    wind_next(1)
+    for j in range(5):
+        at = pl.ds(pl.multiple_of((first + j) * 128, 128), 128)
+        columns(2, j, rates[0:1, at])
+        columns(3, j, rates[1:2, at])
     load_a.wait()
     load_b.wait()
+    wind_next(2)
 
     def returning(i, c):
         h = lax.rem(z + i + 1, 4)
@@ -453,8 +454,8 @@
         means = jnp.sum(inc[STEP + 8 : STEP + 11, :], axis=0, keepdims=True)
         m0 = means[:, 0:COLS]
         m1 = means[:, COLS:CELLS]
-        w0 = wind_row(r0)
-        w1 = wind_row(r0 + 1)
+        w0 = winds[pl.ds(r0, 1), :]
+        w1 = winds[pl.ds(r0 + 1, 1), :]
 
         def step(i, carry):
             here = pl.ds(pl.multiple_of(i * SUB, SUB), SUB)
@@ -472,8 +473,10 @@
 
         lax.fori_loop(0, count, step, 0, unroll=4)
 
+    for r in range(ROWS):
+        winds[r : r + 1, :] = wind_row(r)
     finish(z, back)
-    for i in range(3):
+    for i in (0, 2, 1):
         for c in range(len(parts)):
             homing(c, i).wait_recv()
         finish(lax.rem(z + i + 1, 4), got)
@@ -526,6 +529,7 @@
             pltpu.VMEM((2, 4, 4, 4, 1, 128), F32),
             pltpu.VMEM((4, 4, 4, 2, 1, 128), F32),
             pltpu.VMEM((128, 128), F32),
+            pltpu.VMEM((ROWS, COLS), F32),
             dma((4,)),
             dma((2,)),
             dma((n, 3)),

time: 49.8 us -> 49.5 us (level)
  the two profiles are of different devices: /device:TPU:88 before, /device:TPU:0 now
where the time goes in v4:
time: 49.5 us; the launch traced here: 49.4 us
  Pallas kernels  46.6 us (94%)
  local copies, waits for them, and re-layouts  1.87 us (4%)
  between operations  0.7 us (1%)
    pallas_call x1, Pallas kernels, coupled(): pl.pallas_call(functools.partial(kernel, cap, parts), out_shape=[pltpu.VM...  46.6 us
    unnamed x13, local copies, waits for them, and re-layouts  1.87 us

profile of v4, /device:TPU:0, one launch (start us, length us, event | category | flops | bytes accessed | tf_op | source)
XLA Modules:
  0.0 49.4 jit_solution(4263286581276008416)
XLA Ops:
  0.0 0.0 copy-start
  0.0 0.0 copy-start.1
  0.0 0.0 copy-start.2
  0.0 0.0 copy-start.3
  0.0 0.0 copy-start.4
  0.0 0.0 copy-start.5
  0.0 46.6 %coupled384.1 = (f32[450,8,256]{2,1,0:T(8,128)S(1)}, s32[1]{0:T(128)}) custom-call(f32[450,8,256]{2,1,0:T(8,128)} %spec.1, bf16[1800,1800]{1,0:T(8,128)(2,1)} %quad_a.1, bf16[1800,1800]{1,0:T(8,128)(2,1)} %quad_b.1, f32[50]{0:T(128)} %speed.1, f32[1800]{0:T(1024)} %growth.1, f32[1800]{0:T(1024)} %dissip.1, f32[1,512]{1,0:T(1,128)} %wind.1, s32[8,256]{1,0:T(8,128)} %slot.1), custom_call_target="tpu_custom_call" | custom-call | tf_op jit(solution)/shard_map/coupled384/pallas_call | solution.py:497
  47.2 0.0 copy-done
  47.2 0.0 copy-done.1
  47.2 0.0 copy-done.2
  47.2 0.0 copy-done.3
  47.3 0.0 copy-done.4
  47.3 0.0 copy-done.5
  47.3 0.2 conditional.1
  47.5 1.8 %copy.14 = f32[450,8,256]{2,1,0:T(8,128)} copy(f32[450,8,256]{2,1,0:T(8,128)S(1)} %get-tuple-element.38) | data formatting | bytes 7372800
Async XLA Ops:
  0.0 47.2 %copy-start = (f32[450,8,256]{2,1,0:T(8,128)S(1)}, f32[450,8,256]{2,1,0:T(8,128)}, u32[]{:S(2)}) copy-start(f32[450,8,256]{2,1,0:T(8,128)} %spec.1) | copy-start | bytes 11059204
  0.0 47.2 %copy-start.1 = (f32[1800]{0:T(1024)S(1)}, f32[1800]{0:T(1024)}, u32[]{:S(2)}) copy-start(f32[1800]{0:T(1024)} %growth.1) | copy-start | bytes 21604
  0.0 47.2 %copy-start.2 = (f32[1800]{0:T(1024)S(1)}, f32[1800]{0:T(1024)}, u32[]{:S(2)}) copy-start(f32[1800]{0:T(1024)} %dissip.1) | copy-start | bytes 21604
  0.0 47.2 %copy-start.3 = (s32[8,256]{1,0:T(8,128)S(1)}, s32[8,256]{1,0:T(8,128)}, u32[]{:S(2)}) copy-start(s32[8,256]{1,0:T(8,128)} %slot.1) | copy-start | bytes 24580
  0.0 47.2 %copy-start.4 = (f32[1,512]{1,0:T(1,128)S(1)}, f32[1,512]{1,0:T(1,128)}, u32[]{:S(2)}) copy-start(f32[1,512]{1,0:T(1,128)} %wind.1) | copy-start | bytes 6148
  0.0 47.3 %copy-start.5 = (f32[50]{0:T(128)S(1)}, f32[50]{0:T(128)}, u32[]{:S(2)}) copy-start(f32[50]{0:T(128)} %speed.1) | copy-start | bytes 604
